TPU v7x, 256 devices: a whole 4x4x8 slice. The times are simulated.
256 devices in a mesh: head: 4 (over x), ctx: 64 (over y, z, core).
Axes of the slice: x: 4, y: 4, z: 8, core: 2. Of those that a mesh axis runs over, the one named last changes fastest.
Arguments:
- queries: bfloat16 [256, 8192], P(('head', 'ctx')), may hold values from -2.5 to 2.5
- d_out: bfloat16 [256, 8192], P(('head', 'ctx')), may hold values from -384 to 384
- out_rows: bfloat16 [256, 8192], P(('head', 'ctx')), may hold values from -6 to 6
- lse: bfloat16 [256, 64], P(('head', 'ctx')), may hold values from 9 to 12
- lengths: int32 [4], replicated, may hold values from 1 to 64, 160 in all
- keys: bfloat16 [131072, 1024], P('ctx', 'head'), may hold values from -2.5 to 2.5
- values: bfloat16 [131072, 1024], P('ctx', 'head'), may hold values from -6 to 6
Outputs:
- d_queries: bfloat16 [256, 8192], P(('head', 'ctx'))
- d_keys: bfloat16 [131072, 1024], P('ctx', 'head')
- d_values: bfloat16 [131072, 1024], P('ctx', 'head')
Inputs may be any that keep to these rules, and one draw needn't show every extreme that they name: lengths of samples; they sum to exactly 160 and the largest is exactly 64.
All inputs are finite; a program needn't handle non-finite values.
Results may differ from a plain program's by a relative error of at most 0.0085.
Values may be sent and summed in bfloat16 or wider, within the bound.
A program may use at most 128 MiB of HBM per device.

v0:
```python
import functools
import math

import jax
import jax.numpy as jnp
from jax import lax
from jax.experimental import pallas as pl
from jax.experimental.pallas import tpu as pltpu
from jax.sharding import PartitionSpec as P

DH = 128
CORES = 2
RING = 8
SLOTS = 12
TILE = 512
LOG2E = math.log2(math.e)
MESH = pl.DeviceIdType.MESH
F32 = jnp.float32
BF16 = jnp.bfloat16
NT = (((1,), (1,)), ((), ()))
TN = (((0,), (0,)), ((), ()))


def kernel(
    nx, ny, nz, slots, tile,
    len_ref, q_ref, m_ref, o_ref, lse_ref, k_hbm, v_hbm,
    dq_ref, dk_out, dv_out,
    k_ref, v_ref, dk_give, dv_give, dk_got, dv_got,
    send_rows, send_stats, recv_rows, recv_stats,
    rows_all, stats_all,
    q_all, m_all, stat_all, probs, d_scores, dq_half, dq_own,
    z_send, z_recv, reduced, back_send, back_recv,
    load_sem, kv_send, kv_recv, give_send, give_recv,
    xy_send, xy_recv, xys_send, xys_recv,
    ring_send, ring_recv, rings_send, rings_recv,
    z_ssem, z_rsem, back_ssem, back_rsem,
):
    x = lax.axis_index("head")
    c = lax.axis_index("ctx")
    core = lax.rem(c, CORES)
    z = lax.rem(lax.div(c, CORES), nz)
    y = lax.div(c, CORES * nz)
    other = 1 - core
    half = nz // 2
    ctx_len = k_ref.shape[1]
    unit = slots * 8
    scale = 1.0 / DH**0.5

    def device(x_to, y_to, z_to, core_to):
        return (x_to, (y_to * nz + z_to) * CORES + core_to)

    def at_z(offset):
        return lax.rem(z + offset + 2 * nz, nz)

    xy_offsets = [(dx, dy) for dx in range(nx) for dy in range(ny) if (dx, dy) != (0, 0)]

    def xy_to(dx, dy):
        return lax.rem(x + dx, nx), lax.rem(y + dy, ny)

    def xy_from(dx, dy):
        return lax.rem(x - dx + nx, nx), lax.rem(y - dy + ny, ny)

    load_k = pltpu.make_async_copy(k_hbm, k_ref.at[0], load_sem.at[0])
    load_v = pltpu.make_async_copy(v_hbm, v_ref.at[0], load_sem.at[1])
    load_k.start()
    load_v.start()

    barrier = pltpu.get_barrier_semaphore()
    partners = [device(*xy_to(dx, dy), z, core) for dx, dy in xy_offsets]
    partners += [device(x, y, at_z(dz), core) for dz in sorted({1, nz - 1})]
    partners += [device(x, y, z, other)]
    for partner in partners:
        pl.semaphore_signal(barrier, inc=1, device_id=partner, device_id_type=MESH)

    heads = nx * 16
    row = lax.broadcasted_iota(jnp.int32, (heads, 128), 0)
    lane = lax.broadcasted_iota(jnp.int32, (heads, 128), 1)
    q_heads = q_ref[...].astype(F32).reshape(heads, DH)
    m_heads = m_ref[...].astype(F32).reshape(heads, DH)
    o_heads = o_ref[...].astype(F32).reshape(heads, DH)
    delta = jnp.sum(m_heads * o_heads, axis=1, keepdims=True)
    lse_row = lse_ref[...].astype(F32) * LOG2E
    square_row = lax.broadcasted_iota(jnp.int32, (heads, heads), 0)
    square_lane = lax.broadcasted_iota(jnp.int32, (heads, heads), 1)
    lse_col = jnp.sum(
        jnp.where(square_row == square_lane, jnp.broadcast_to(lse_row, (heads, heads)), 0.0),
        axis=1, keepdims=True,
    )
    diagonal = lax.rem(lane, 8) == lax.rem(row, 8)

    def along_lanes(column):
        spread = jnp.where(diagonal, jnp.broadcast_to(column, (heads, 128)), 0.0)
        return jnp.sum(spread.reshape(heads // 8, 8, 128), axis=1)

    lse_lanes = along_lanes(lse_col)
    delta_lanes = along_lanes(delta)
    for i in range(nx):
        send_rows[i, 0:16, :] = q_heads[16 * i : 16 * i + 16].astype(BF16)
        send_rows[i, 16:32, :] = m_heads[16 * i : 16 * i + 16].astype(BF16)
        for g in range(2):
            send_stats[i, 2 * g : 2 * g + 1, :] = lse_lanes[2 * i + g : 2 * i + g + 1]
            send_stats[i, 2 * g + 1 : 2 * g + 2, :] = delta_lanes[2 * i + g : 2 * i + g + 1]

    pl.semaphore_wait(barrier, len(partners))

    mine = x * ny + y

    def xy_copies(i, dx, dy):
        x_to, y_to = xy_to(dx, dy)
        to = device(x_to, y_to, z, core)
        return (
            pltpu.make_async_remote_copy(
                src_ref=send_rows.at[x_to], dst_ref=recv_rows.at[mine],
                send_sem=xy_send.at[i], recv_sem=xy_recv.at[i],
                device_id=to, device_id_type=MESH,
            ),
            pltpu.make_async_remote_copy(
                src_ref=send_stats.at[x_to], dst_ref=recv_stats.at[mine],
                send_sem=xys_send.at[i], recv_sem=xys_recv.at[i],
                device_id=to, device_id_type=MESH,
            ),
        )

    pending = []
    for i, (dx, dy) in enumerate(xy_offsets):
        for copy in xy_copies(i, dx, dy):
            copy.start()
            pending.append(copy)
    sibling = device(x, y, z, other)

    def to_sibling(source, target, send, recv):
        return pltpu.make_async_remote_copy(
            src_ref=source, dst_ref=target, send_sem=send, recv_sem=recv,
            device_id=sibling, device_id_type=MESH,
        )

    shared = [
        to_sibling(source, target.at[1], kv_send.at[i], kv_recv.at[i])
        for i, (source, target) in enumerate(((k_hbm, k_ref), (v_hbm, v_ref)))
    ]
    for copy in shared:
        copy.start()
    recv_rows[mine] = send_rows[x]
    recv_stats[mine] = send_stats[x]
    q_all[...] = jnp.zeros_like(q_all)
    m_all[...] = jnp.zeros_like(m_all)
    for copy in pending:
        copy.wait_recv()

    stride = nz * CORES
    place = z * CORES + core
    starts, counts = [], []
    total = jnp.int32(0)
    for h in range(nx):
        live = lax.div(len_ref[h] - place + (stride - 1), stride)
        live = jnp.minimum(jnp.maximum(live, 0), ny)
        starts.append(total)
        counts.append(live)
        total = total + live

    stat_lane = lax.broadcasted_iota(jnp.int32, (4, 128), 1)

    def slot_rows(s):
        sample = jnp.int32(0)
        first = jnp.int32(0)
        for h in range(1, nx):
            past = s >= starts[h]
            sample = jnp.where(past, h, sample)
            first = jnp.where(past, starts[h], first)
        valid = s < total
        index = jnp.where(valid, sample * ny + (s - first), 0)
        packet = recv_rows[index].astype(F32).reshape(4, 8, 128)
        packet = jnp.where(valid, packet, 0.0)
        stat = jnp.where(jnp.logical_and(lax.div(stat_lane, 8) == s, valid), recv_stats[index], 0.0)
        return packet, stat

    stats = jnp.zeros((4, 128), F32)
    for s in range(0, slots, 2):
        first, stat = slot_rows(s)
        second, stat_second = slot_rows(s + 1)
        stats = stats + stat + stat_second
        for part in range(2):
            for g in range(2):
                both = jnp.concatenate([first[2 * part + g], second[2 * part + g]], axis=0)
                rows_all[z, part, g, 8 * s : 8 * s + 16, :] = both.astype(BF16)
    stats_all[z] = stats

    def when(condition, action):
        if isinstance(condition, bool):
            if condition:
                action()
        else:
            pl.when(condition)(action)

    def start(copies):
        for copy in copies:
            copy.start()

    def ring_copies(direction, hop, part, arriving=False):
        step = 1 if direction == 0 else -1
        block = at_z(-step * (hop if arriving else hop - 1))
        to = device(x, y, at_z(step), core)
        copies = [
            pltpu.make_async_remote_copy(
                src_ref=rows_all.at[block, part], dst_ref=rows_all.at[block, part],
                send_sem=ring_send.at[direction, hop, part],
                recv_sem=ring_recv.at[direction, hop, part],
                device_id=to, device_id_type=MESH,
            )
        ]
        if part == 0:
            copies.append(
                pltpu.make_async_remote_copy(
                    src_ref=stats_all.at[block], dst_ref=stats_all.at[block],
                    send_sem=rings_send.at[direction, hop], recv_sem=rings_recv.at[direction, hop],
                    device_id=to, device_id_type=MESH,
                )
            )
        return copies

    def advance(part, hop):
        for copy in ring_copies(0, hop, part, arriving=True):
            copy.wait_recv()
        when(hop < half, lambda: start(ring_copies(0, hop + 1, part)))

        def leftward():
            for copy in ring_copies(1, hop, part, arriving=True):
                copy.wait_recv()
            when(hop + 1 < half, lambda: start(ring_copies(1, hop + 1, part)))

        when(hop < half, leftward)

    block_width = 2 * unit
    middle_width = 2 * block_width
    own_at = (half - 1) * middle_width
    far_at = own_at + block_width
    columns = far_at + block_width
    far_from = far_at // 128 * 128

    def gather(offsets, at):
        for part, held in enumerate((q_all, m_all)):
            for n, offset in enumerate(offsets):
                for g in range(2):
                    to = at + n * block_width + g * unit
                    if not isinstance(to, int):
                        to = pl.multiple_of(to, 16)
                    held[pl.ds(to, unit), g * DH : (g + 1) * DH] = rows_all[at_z(offset), part, g]

    def stat_lanes(offsets):
        pieces = [
            stats_all[at_z(offset)][2 * g : 2 * g + 2, :unit]
            for offset in offsets for g in range(2)
        ]
        return jnp.concatenate(pieces, axis=1)

    def front(at, width, side):
        if isinstance(at, int):
            here = pl.ds(at, width)
        else:
            here = pl.ds(pl.multiple_of(at, 128), width)
        k = k_ref[side]
        scores = lax.dot_general(k, q_all[here, :], NT, preferred_element_type=F32)
        weights = jnp.exp2(scores * (scale * LOG2E) - stat_all[0:1, here])
        probs[side, :, here] = weights.astype(BF16)
        d_weights = lax.dot_general(v_ref[side], m_all[here, :], NT, preferred_element_type=F32)
        d_score = (weights * (d_weights - stat_all[1:2, here])).astype(BF16)
        d_scores[side, :, here] = d_score
        return lax.dot_general(d_score, k, TN, preferred_element_type=F32)

    def back(side, index):
        here = pl.ds(pl.multiple_of(index * tile, tile), tile)
        d_v = jnp.dot(probs[side, here, :], m_all[...], preferred_element_type=F32)
        d_k = jnp.dot(d_scores[side, here, :], q_all[...], preferred_element_type=F32)
        return here, d_v, d_k

    def z_copy(offset):
        return pltpu.make_async_remote_copy(
            src_ref=z_send.at[offset], dst_ref=z_recv.at[offset],
            send_sem=z_ssem.at[offset], recv_sem=z_rsem.at[offset],
            device_id=device(x, y, at_z(offset), core), device_id_type=MESH,
        )

    def give(offsets, d_query):
        for n, offset in enumerate(offsets):
            for g in range(2):
                low = n * block_width + g * unit
                z_send[offset, g] = d_query[low : low + unit, g * DH : (g + 1) * DH].astype(BF16)
            z_copy(offset).start()

    for part in range(2):
        start(ring_copies(0, 1, part))
        if half > 1:
            start(ring_copies(1, 1, part))
    gather([0], own_at)
    stat_all[:, own_at:far_at] = stat_lanes([0])
    load_k.wait()
    load_v.wait()
    d_query = front(own_at, block_width, 0)
    for g in range(2):
        dq_own[g] = d_query[g * unit : (g + 1) * unit, g * DH : (g + 1) * DH]
    for copy in shared:
        copy.wait_recv()
    d_query = front(own_at, block_width, 1)
    for g in range(2):
        dq_own[g] += d_query[g * unit : (g + 1) * unit, g * DH : (g + 1) * DH]
    advance(0, 1)
    advance(1, 1)

    def middle(hop, carry):
        offsets = [hop, nz - hop]
        at = (hop - 1) * middle_width
        gather(offsets, at)
        stat_all[:, pl.ds(pl.multiple_of(at, 128), middle_width)] = stat_lanes(offsets)
        dq_half[...] = front(at, middle_width, 0)
        advance(0, hop + 1)
        dq_half[...] += front(at, middle_width, 1)
        advance(1, hop + 1)
        give(offsets, dq_half[...])
        return carry

    lax.fori_loop(1, half, middle, 0)

    gather([half], far_at)
    stat_all[:, own_at:columns] = stat_lanes([0, half])
    far_width = columns - far_from
    dq_half[0:far_width] = front(far_from, far_width, 0)
    d_query = dq_half[0:far_width] + front(far_from, far_width, 1)
    give([half], d_query[far_at - far_from :])

    tiles = ctx_len // tile

    def give_copies(index):
        here = pl.ds(pl.multiple_of(index * tile, tile), tile)
        return (
            to_sibling(dv_give.at[here], dv_got.at[here], give_send.at[0, index], give_recv.at[0, index]),
            to_sibling(dk_give.at[here], dk_got.at[here], give_send.at[1, index], give_recv.at[1, index]),
        )

    def give_tile(index, carry):
        here, d_v, d_k = back(1, index)
        dv_give[here, :] = d_v.astype(BF16)
        dk_give[here, :] = d_k.astype(BF16)
        start(give_copies(index))
        return carry

    def own_tile(index, carry):
        here, d_v, d_k = back(0, index)
        for copy in give_copies(index):
            copy.wait_recv()
        dv_out[here, :] = (d_v + dv_got[here, :].astype(F32)).astype(BF16)
        dk_out[here, :] = ((d_k + dk_got[here, :].astype(F32)) * scale).astype(BF16)
        return carry

    lax.fori_loop(0, tiles, give_tile, 0)
    lax.fori_loop(0, tiles // 4, own_tile, 0)

    result = dq_own[...]
    for offset in range(1, nz):
        z_copy(offset).wait_recv()
        result = result + z_recv[offset].astype(F32)
    for g in range(2):
        reduced[:, 8 * g : 8 * g + 8, :] = result[g].reshape(slots, 8, 128)

    for h in range(nx):
        for row_y in range(ny):
            valid = row_y < counts[h]
            slot = jnp.where(valid, starts[h] + row_y, 0)
            back_send[h * ny + row_y] = jnp.where(valid, reduced[slot], 0.0).astype(BF16)

    def back_copy(i, dx, dy):
        x_to, y_to = xy_to(dx, dy)
        return pltpu.make_async_remote_copy(
            src_ref=back_send.at[x_to * ny + y_to], dst_ref=back_recv.at[mine],
            send_sem=back_ssem.at[i], recv_sem=back_rsem.at[i],
            device_id=device(x_to, y_to, z, core), device_id_type=MESH,
        )

    backs = [back_copy(i, dx, dy) for i, (dx, dy) in enumerate(xy_offsets)]
    start(backs)
    back_recv[mine] = back_send[mine]
    lax.fori_loop(tiles // 4, tiles, own_tile, 0)
    for copy in backs:
        copy.wait_recv()
    for i in range(nx):
        owned = back_recv[i * ny].astype(F32)
        for row_y in range(1, ny):
            owned = owned + back_recv[i * ny + row_y].astype(F32)
        dq_ref[:, 16 * DH * i : 16 * DH * (i + 1)] = (owned * scale).reshape(1, 16 * DH).astype(BF16)

    for copy in pending + backs + shared:
        copy.wait_send()
    for part in range(2):
        for hop in range(1, half + 1):
            for copy in ring_copies(0, hop, part):
                copy.wait_send()
            if hop < half:
                for copy in ring_copies(1, hop, part):
                    copy.wait_send()
    for offset in range(1, nz):
        z_copy(offset).wait_send()

    def gave(index, carry):
        for copy in give_copies(index):
            copy.wait_send()
        return carry

    lax.fori_loop(0, tiles, gave, 0)


def fused(nx, ny, nz, slots, tile, lengths, q, m, o, lse, keys, values):
    ctx_len, kv_cols = keys.shape
    unit = slots * 8
    columns = 2 * nz * unit
    vmem = pl.BlockSpec(memory_space=pltpu.VMEM)
    smem = pl.BlockSpec(memory_space=pltpu.SMEM)
    hbm = pl.BlockSpec(memory_space=pl.ANY)
    dma = pltpu.SemaphoreType.DMA
    packets = nx * ny
    half = nz // 2
    tiles = ctx_len // tile
    scratch = [
        pltpu.VMEM((CORES, ctx_len, kv_cols), BF16),
        pltpu.VMEM((CORES, ctx_len, kv_cols), BF16),
    ] + [pltpu.VMEM((ctx_len, kv_cols), BF16)] * 4 + [
        pltpu.VMEM((nx, 32, 128), BF16),
        pltpu.VMEM((nx, 4, 128), F32),
        pltpu.VMEM((packets, 32, 128), BF16),
        pltpu.VMEM((packets, 4, 128), F32),
        pltpu.VMEM((nz, 2, 2, unit, 128), BF16),
        pltpu.VMEM((nz, 4, 128), F32),
        pltpu.VMEM((columns, kv_cols), BF16),
        pltpu.VMEM((columns, kv_cols), BF16),
        pltpu.VMEM((2, columns), F32),
        pltpu.VMEM((CORES, ctx_len, columns), BF16),
        pltpu.VMEM((CORES, ctx_len, columns), BF16),
        pltpu.VMEM((4 * unit, kv_cols), F32),
        pltpu.VMEM((2, unit, 128), F32),
        pltpu.VMEM((nz, 2, unit, 128), BF16),
        pltpu.VMEM((nz, 2, unit, 128), BF16),
        pltpu.VMEM((slots, 16, 128), F32),
        pltpu.VMEM((packets, 16, 128), BF16),
        pltpu.VMEM((packets, 16, 128), BF16),
        dma((2,)), dma((2,)), dma((2,)), dma((2, tiles)), dma((2, tiles)),
        dma((packets,)), dma((packets,)), dma((packets,)), dma((packets,)),
        dma((2, half + 1, 2)), dma((2, half + 1, 2)), dma((2, half + 1)), dma((2, half + 1)),
        dma((nz,)), dma((nz,)),
        dma((packets,)), dma((packets,)),
    ]
    flops = 5 * 2 * ctx_len * 128 * 2 * unit * 2 * nz
    return pl.pallas_call(
        functools.partial(kernel, nx, ny, nz, slots, tile),
        out_shape=(
            jax.ShapeDtypeStruct(q.shape, BF16),
            pltpu.VMEM(keys.shape, BF16),
            pltpu.VMEM(values.shape, BF16),
        ),
        in_specs=[smem, vmem, vmem, vmem, vmem, hbm, hbm],
        out_specs=(vmem, vmem, vmem),
        scratch_shapes=scratch,
        compiler_params=pltpu.CompilerParams(
            collective_id=0, has_side_effects=True, vmem_limit_bytes=56 << 20
        ),
        cost_estimate=pl.CostEstimate(
            flops=flops, bytes_accessed=8 * ctx_len * kv_cols, transcendentals=0
        ),
    )(lengths, q, m, o, lse, keys, values)


def hand_over_kernel(dq_in, dk_in, dv_in, dq_out, dk_out, dv_out, sems):
    copies = [
        pltpu.make_async_copy(dk_in, dk_out, sems.at[0]),
        pltpu.make_async_copy(dv_in, dv_out, sems.at[1]),
    ]
    for copy in copies:
        copy.start()
    dq_out[...] = dq_in[...]
    for copy in copies:
        copy.wait()


def hand_over(d_q, d_k, d_v):
    vmem = pl.BlockSpec(memory_space=pltpu.VMEM)
    hbm = pl.BlockSpec(memory_space=pl.ANY)
    return pl.pallas_call(
        hand_over_kernel,
        out_shape=tuple(
            pltpu.HBM(a.shape, a.dtype) if i else jax.ShapeDtypeStruct(a.shape, a.dtype)
            for i, a in enumerate((d_q, d_k, d_v))
        ),
        in_specs=[vmem, vmem, vmem],
        out_specs=(vmem, hbm, hbm),
        scratch_shapes=[pltpu.SemaphoreType.DMA((2,))],
        compiler_params=pltpu.CompilerParams(vmem_limit_bytes=8 << 20),
    )(d_q, d_k, d_v)


def solution(mesh, nz=RING, slots=SLOTS, tile=TILE):
    nx = mesh.shape["head"]
    ny = mesh.shape["ctx"] // (nz * CORES)

    def on_device(queries, d_out, out_rows, lse, lengths, keys, values):
        d_q, d_k, d_v = fused(
            nx, ny, nz, slots, tile, lengths,
            queries, d_out, out_rows, lse, keys, values,
        )
        return hand_over(d_q, d_k, d_v)

    rows = P(("head", "ctx"), None)
    return jax.shard_map(
        on_device,
        mesh=mesh,
        in_specs=(rows, rows, rows, rows, P(), P("ctx", "head"), P("ctx", "head")),
        out_specs=(rows, P("ctx", "head"), P("ctx", "head")),
        check_vma=False,
    )
```

profile of v0, /device:TPU:8, one launch (start us, length us, event | category | flops | bytes accessed | tf_op | source)
XLA Modules:
  0.0 53.1 jit_solution(5903182977549728116)
XLA Ops:
  0.6 49.7 %shard_map.94 = (bf16[1,8192]{1,0:T(2,128)(2,1)}, bf16[2048,256]{1,0:T(8,128)(2,1)S(1)}, bf16[2048,256]{1,0:T(8,128)(2,1)S(1)}) custom-call(s32[4]{0:T(128)} %len_ref.1, bf16[1,8192]{1,0:T(2,128)(2,1)} %q_ref.1, bf16[1,8192]{1,0:T(2,128)(2,1)} %m_ref.1, bf16[1,8192]{1,0:T(2,128)(2,1)} %o_ref.1, bf16[1,64]{1,0:T(2,128)(2,1)} %lse_ref.1, ...), custom_call_target="tpu_custom_call" | custom-call | flops 8053063680 | bytes 4194304 | tf_op jit(solution)/shard_map/pallas_call | solution.py:450
  50.4 0.0 copy-start
  50.4 0.7 %copy-done = bf16[1,8192]{1,0:T(2,128)(2,1)S(1)} copy-done((bf16[1,8192]{1,0:T(2,128)(2,1)S(1)}, bf16[1,8192]{1,0:T(2,128)(2,1)}, u32[]{:S(2)}) %copy-start) | copy-done | bytes 16408
  51.1 1.9 %shard_map.95 = (bf16[1,8192]{1,0:T(2,128)(2,1)}, bf16[2048,256]{1,0:T(8,128)(2,1)}, bf16[2048,256]{1,0:T(8,128)(2,1)}) custom-call(bf16[1,8192]{1,0:T(2,128)(2,1)S(1)} %copy-done, bf16[2048,256]{1,0:T(8,128)(2,1)S(1)} %get-tuple-element.7.dk_in, bf16[2048,256]{1,0:T(8,128)(2,1)S(1)} %get-tuple-element.8.dv_in), custom_call_target="tpu_custom_call" | custom-call | tf_op jit(solution)/shard_map/pallas_call | solution.py:484
Async XLA Ops:
  50.4 0.8 %copy-start = (bf16[1,8192]{1,0:T(2,128)(2,1)S(1)}, bf16[1,8192]{1,0:T(2,128)(2,1)}, u32[]{:S(2)}) copy-start(bf16[1,8192]{1,0:T(2,128)(2,1)} %get-tuple-element.6.dq_in) | copy-start | bytes 49156
where the time goes:
time: 53.3 us; the launch traced here: 53.1 us
  Pallas kernels  51.7 us (97%)
  local copies, waits for them, and re-layouts  0.75 us (1%)
  between operations  0.65 us (1%)
    pallas_call x1, Pallas kernels, fused(): pl.pallas_call(functools.partial(kernel, nx, ny, nz, slots, tile), out_sh...  49.7 us
    pallas_call x1, Pallas kernels, hand_over(): pl.pallas_call(hand_over_kernel, out_shape=tuple((pltpu.HBM(a.shape, a.dt...  1.94 us

commit v1 on v0

--- a/solution.py
+++ b/solution.py
@@ -160,7 +160,8 @@
 
     stat_lane = lax.broadcasted_iota(jnp.int32, (4, 128), 1)
 
-    def slot_rows(s):
+    picks = []
+    for s in range(slots):
         sample = jnp.int32(0)
         first = jnp.int32(0)
         for h in range(1, nx):
@@ -168,22 +169,24 @@
             sample = jnp.where(past, h, sample)
             first = jnp.where(past, starts[h], first)
         valid = s < total
-        index = jnp.where(valid, sample * ny + (s - first), 0)
-        packet = recv_rows[index].astype(F32).reshape(4, 8, 128)
-        packet = jnp.where(valid, packet, 0.0)
-        stat = jnp.where(jnp.logical_and(lax.div(stat_lane, 8) == s, valid), recv_stats[index], 0.0)
-        return packet, stat
-
-    stats = jnp.zeros((4, 128), F32)
-    for s in range(0, slots, 2):
-        first, stat = slot_rows(s)
-        second, stat_second = slot_rows(s + 1)
-        stats = stats + stat + stat_second
-        for part in range(2):
+        picks.append((valid, jnp.where(valid, sample * ny + (s - first), 0)))
+
+    def fill_stats():
+        stats = jnp.zeros((4, 128), F32)
+        for s, (valid, index) in enumerate(picks):
+            ours = jnp.logical_and(lax.div(stat_lane, 8) == s, valid)
+            stats = stats + jnp.where(ours, recv_stats[index], 0.0)
+        stats_all[z] = stats
+
+    def fill_rows(part):
+        for s in range(0, slots, 2):
+            pair = []
+            for valid, index in picks[s : s + 2]:
+                packet = recv_rows[index, 16 * part : 16 * part + 16, :].astype(F32)
+                pair.append(jnp.where(valid, packet, 0.0))
             for g in range(2):
-                both = jnp.concatenate([first[2 * part + g], second[2 * part + g]], axis=0)
+                both = jnp.concatenate([rows[8 * g : 8 * g + 8] for rows in pair], axis=0)
                 rows_all[z, part, g, 8 * s : 8 * s + 16, :] = both.astype(BF16)
-    stats_all[z] = stats
 
     def when(condition, action):
         if isinstance(condition, bool):
@@ -288,6 +291,9 @@
             z_copy(offset).start()
 
     for part in range(2):
+        if part == 0:
+            fill_stats()
+        fill_rows(part)
         start(ring_copies(0, 1, part))
         if half > 1:
             start(ring_copies(1, 1, part))
@@ -379,15 +385,8 @@
     start(backs)
     back_recv[mine] = back_send[mine]
     lax.fori_loop(tiles // 4, tiles, own_tile, 0)
-    for copy in backs:
-        copy.wait_recv()
-    for i in range(nx):
-        owned = back_recv[i * ny].astype(F32)
-        for row_y in range(1, ny):
-            owned = owned + back_recv[i * ny + row_y].astype(F32)
-        dq_ref[:, 16 * DH * i : 16 * DH * (i + 1)] = (owned * scale).reshape(1, 16 * DH).astype(BF16)
-
-    for copy in pending + backs + shared:
+
+    for copy in pending + shared:
         copy.wait_send()
     for part in range(2):
         for hop in range(1, half + 1):
@@ -405,6 +404,16 @@
         return carry
 
     lax.fori_loop(0, tiles, gave, 0)
+
+    for copy in backs:
+        copy.wait_recv()
+    for i in range(nx):
+        owned = back_recv[i * ny].astype(F32)
+        for row_y in range(1, ny):
+            owned = owned + back_recv[i * ny + row_y].astype(F32)
+        dq_ref[:, 16 * DH * i : 16 * DH * (i + 1)] = (owned * scale).reshape(1, 16 * DH).astype(BF16)
+    for copy in backs:
+        copy.wait_send()
 
 
 def fused(nx, ny, nz, slots, tile, lengths, q, m, o, lse, keys, values):
@@ -450,7 +459,7 @@
     return pl.pallas_call(
         functools.partial(kernel, nx, ny, nz, slots, tile),
         out_shape=(
-            jax.ShapeDtypeStruct(q.shape, BF16),
+            pltpu.VMEM(q.shape, BF16),
             pltpu.VMEM(keys.shape, BF16),
             pltpu.VMEM(values.shape, BF16),
         ),

time: 53.3 us -> 51.7 us (0.970)
  Pallas kernels: 51.7 us -> 50.9 us
  local copies, waits for them, and re-layouts: 0.75 us -> 0 us
    pallas_call x1, Pallas kernels: 49.7 us -> 48.9 us  [fused(): pl.pallas_call(functools.partial(kernel, nx, ny, nz, slots, tile), out_sh...]
    unnamed x2 -> x0, local copies, waits for them, and re-layouts: 0.75 us -> none
where the time goes in v1:
time: 51.7 us; the launch traced here: 51.5 us
  Pallas kernels  50.9 us (98%)
  between operations  0.64 us (1%)
    pallas_call x1, Pallas kernels, fused(): pl.pallas_call(functools.partial(kernel, nx, ny, nz, slots, tile), out_sh...  48.9 us
    pallas_call x1, Pallas kernels, hand_over(): pl.pallas_call(hand_over_kernel, out_shape=tuple((pltpu.HBM(a.shape, a.dt...  1.95 us

profile of v1, /device:TPU:8, one launch (start us, length us, event | category | flops | bytes accessed | tf_op | source)
XLA Modules:
  0.0 51.5 jit_solution(17691366271807262008)
XLA Ops:
  0.6 48.9 %shard_map.94 = (bf16[1,8192]{1,0:T(2,128)(2,1)S(1)}, bf16[2048,256]{1,0:T(8,128)(2,1)S(1)}, bf16[2048,256]{1,0:T(8,128)(2,1)S(1)}) custom-call(s32[4]{0:T(128)} %len_ref.1, bf16[1,8192]{1,0:T(2,128)(2,1)} %q_ref.1, bf16[1,8192]{1,0:T(2,128)(2,1)} %m_ref.1, bf16[1,8192]{1,0:T(2,128)(2,1)} %o_ref.1, bf16[1,64]{1,0:T(2,128)(2,1)} %lse_ref.1, ...), custom_call_target="tpu_custom_call" | custom-call | flops 8053063680 | bytes 4194304 | tf_op jit(solution)/shard_map/pallas_call | solution.py:459
  49.6 1.9 %shard_map.95 = (bf16[1,8192]{1,0:T(2,128)(2,1)}, bf16[2048,256]{1,0:T(8,128)(2,1)}, bf16[2048,256]{1,0:T(8,128)(2,1)}) custom-call(bf16[1,8192]{1,0:T(2,128)(2,1)S(1)} %get-tuple-element.6.dq_in, bf16[2048,256]{1,0:T(8,128)(2,1)S(1)} %get-tuple-element.7.dk_in, bf16[2048,256]{1,0:T(8,128)(2,1)S(1)} %get-tuple-element.8.dv_in), custom_call_target="tpu_custom_call" | custom-call | tf_op jit(solution)/shard_map/pallas_call | solution.py:493

commit v2 on v1

--- a/solution.py
+++ b/solution.py
@@ -52,7 +52,11 @@
     def at_z(offset):
         return lax.rem(z + offset + 2 * nz, nz)
 
+    def hops(offset):
+        return min(offset[0], nx - offset[0]) + min(offset[1], ny - offset[1])
+
     xy_offsets = [(dx, dy) for dx in range(nx) for dy in range(ny) if (dx, dy) != (0, 0)]
+    xy_offsets.sort(key=hops, reverse=True)
 
     def xy_to(dx, dy):
         return lax.rem(x + dx, nx), lax.rem(y + dy, ny)

time: 51.7 us -> 51 us (0.986)
  Pallas kernels: 50.9 us -> 50 us
    pallas_call x1, Pallas kernels: 48.9 us -> 48.1 us  [fused(): pl.pallas_call(functools.partial(kernel, nx, ny, nz, slots, tile), out_sh...]
where the time goes in v2:
time: 51 us; the launch traced here: 50.6 us
  Pallas kernels  50 us (98%)
  between operations  0.64 us (1%)
    pallas_call x1, Pallas kernels, fused(): pl.pallas_call(functools.partial(kernel, nx, ny, nz, slots, tile), out_sh...  48.1 us
    pallas_call x1, Pallas kernels, hand_over(): pl.pallas_call(hand_over_kernel, out_shape=tuple((pltpu.HBM(a.shape, a.dt...  1.95 us

profile of v2, /device:TPU:8, one launch (start us, length us, event | category | flops | bytes accessed | tf_op | source)
XLA Modules:
  0.0 50.6 jit_solution(5819931697849520865)
XLA Ops:
  0.6 48.1 %shard_map.94 = (bf16[1,8192]{1,0:T(2,128)(2,1)S(1)}, bf16[2048,256]{1,0:T(8,128)(2,1)S(1)}, bf16[2048,256]{1,0:T(8,128)(2,1)S(1)}) custom-call(s32[4]{0:T(128)} %len_ref.1, bf16[1,8192]{1,0:T(2,128)(2,1)} %q_ref.1, bf16[1,8192]{1,0:T(2,128)(2,1)} %m_ref.1, bf16[1,8192]{1,0:T(2,128)(2,1)} %o_ref.1, bf16[1,64]{1,0:T(2,128)(2,1)} %lse_ref.1, ...), custom_call_target="tpu_custom_call" | custom-call | flops 8053063680 | bytes 4194304 | tf_op jit(solution)/shard_map/pallas_call | solution.py:463
  48.7 1.9 %shard_map.95 = (bf16[1,8192]{1,0:T(2,128)(2,1)}, bf16[2048,256]{1,0:T(8,128)(2,1)}, bf16[2048,256]{1,0:T(8,128)(2,1)}) custom-call(bf16[1,8192]{1,0:T(2,128)(2,1)S(1)} %get-tuple-element.6.dq_in, bf16[2048,256]{1,0:T(8,128)(2,1)S(1)} %get-tuple-element.7.dk_in, bf16[2048,256]{1,0:T(8,128)(2,1)S(1)} %get-tuple-element.8.dv_in), custom_call_target="tpu_custom_call" | custom-call | tf_op jit(solution)/shard_map/pallas_call | solution.py:497
